TPU v7x, 32 devices: a whole 2x2x4 slice. The times are simulated.
32 devices in a mesh: clip: 2 (over x), tile: 16 (over z, y, core).
Axes of the slice: x: 2, y: 2, z: 4, core: 2. Of those that a mesh axis runs over, the one named last changes fastest.
Arguments:
- frames: bfloat16 [8, 32, 128, 1024], P('clip', 'tile'), parts along dimension 0, may hold values from -40 to 40
- keyframes: bfloat16 [4, 32, 128, 1024], P('clip', 'tile'), parts along dimension 0, may hold values from -40 to 40
- matches: int32 [16, 8, 4], P('tile', 'clip'), parts along dimension 1, may hold values from 0 to 5, as said below
- counts: int32 [16, 8], P('tile', 'clip'), parts along dimension 1, may hold values from 1 to 4, as said below
- w_query: bfloat16 [1024, 1024], replicated, may hold values from -1 to 1
- w_key: bfloat16 [1024, 1024], replicated, may hold values from -1 to 1
- w_value: bfloat16 [1024, 1024], replicated, may hold values from -0.1875 to 0.1875
- w_out: bfloat16 [1024, 1024], replicated, may hold values from -0.1875 to 0.1875
Outputs:
- mixed: bfloat16 [8, 32, 128, 1024], P('clip', None, 'tile'), parts along dimension 0
There are 2 independent parts, one for each index of `clip`. A program takes and returns all parts, laid end to end along the dimension named above; an argument that names none is the same for every part. Nothing has to cross between parts.
Inputs may be any that keep to these rules, and one draw needn't show every extreme that they name: `matches`: every entry names a candidate whose block lies inside the image; the entries of one list are distinct, and entry 0 is candidate 1 (keyframe 0's block at the reader's own tile). Entries past the count are valid but unused. `counts`: in every frame some tile uses 4 entries.
All inputs are finite; a program needn't handle non-finite values.
Results may differ from a plain program's by a relative error of at most 0.0095.
Values may be sent and summed in bfloat16 or wider, within the bound.
A program may use at most 128 MiB of HBM per device.

v0:
```python
import functools

import jax
import jax.numpy as jnp
from jax import lax
from jax.experimental import pallas as pl
from jax.experimental.pallas import tpu as pltpu
from jax.sharding import PartitionSpec as P

HEADS = 16
PAIR = 128
EARLY_QUERIES = 1
CHUNK = 512
F32 = jnp.float32
BF16 = jnp.bfloat16


def kernel(
    tiles, exchange, col_count,
    matches_in, counts_in, frames_in, keys_in, wq_in, wk_in, wv_in, wo_in,
    out,
    matches, counts, frames, stills, wq, wk, wv, wo, queries, key_table, value_table, context,
    stage, scores_even, scores_odd, max_even, max_odd, early_total, early_max,
    load_sem, halo_send, halo_recv, send_sem, recv_sem, own_sem,
):
    frame_count, block_len, model_dim = frames.shape
    key_count = stills.shape[1] // block_len
    slot_count = matches.shape[2]
    head_dim = model_dim // HEADS
    pair_count = model_dim // PAIR
    chunk_count = model_dim // CHUNK
    rows = block_len // col_count
    cols = col_count // tiles
    me = lax.axis_index("tile")

    loads = [
        pltpu.make_async_copy(src, dst, load_sem.at[i])
        for i, (src, dst) in enumerate(
            [
                (wq_in, wq), (frames_in, frames), (keys_in, stills.at[1]),
                (wk_in, wk), (wv_in, wv), (wo_in, wo),
                (matches_in, matches), (counts_in, counts),
            ]
        )
    ]
    for load in loads:
        load.start()

    barrier = pltpu.get_barrier_semaphore()

    def greet(step, carry):
        other = lax.rem(me + step, tiles)
        pl.semaphore_signal(
            barrier, inc=1, device_id={"tile": other}, device_id_type=pl.DeviceIdType.MESH
        )
        return carry

    lax.fori_loop(1, tiles, greet, 0)
    pl.semaphore_wait(barrier, tiles - 1)

    odd = lax.rem(me, 2)
    partners = ((me + 1 - 2 * odd, 2 - 2 * odd), (me - 1 + 2 * odd, 2 * odd))
    far = partners[1][0]
    has_far = (far >= 0) & (far < tiles)

    def halo(kind, key):
        part = pl.ds(key * block_len, block_len)
        return pltpu.make_async_remote_copy(
            src_ref=keys_in.at[part], dst_ref=stills.at[partners[1 - kind][1], part],
            send_sem=halo_send.at[kind, key], recv_sem=halo_recv.at[kind, key],
            device_id={"tile": partners[kind][0]}, device_id_type=pl.DeviceIdType.MESH,
        )

    def arrival(kind, key):
        part = pl.ds(key * block_len, block_len)
        return pltpu.make_async_remote_copy(
            src_ref=keys_in.at[part], dst_ref=stills.at[partners[kind][1], part],
            send_sem=halo_send.at[kind, key], recv_sem=halo_recv.at[kind, key],
            device_id={"tile": partners[kind][0]}, device_id_type=pl.DeviceIdType.MESH,
        )

    @pl.when(has_far)
    def _():
        for key in range(key_count):
            halo(1, key).start()

    for key in range(key_count):
        halo(0, key).start()

    def fill(block, carry):
        one = jnp.where(block < 3 * key_count, 1.0, 0.0).astype(BF16)
        for pair in range(pair_count):
            value_table[block, :, pl.ds(pair * 2 * PAIR + PAIR, PAIR)] = jnp.full(
                (block_len, PAIR), 1.0, F32
            ).astype(BF16) * one
        return carry

    lax.fori_loop(0, 3 * key_count + 1, fill, 0)
    for pair in range(pair_count):
        value_table[3 * key_count, :, pl.ds(pair * 2 * PAIR, PAIR)] = jnp.zeros(
            (block_len, PAIR), BF16
        )

    loads[0].wait()
    loads[1].wait()
    lane = lax.broadcasted_iota(jnp.int32, (block_len, CHUNK), 1)
    even = lax.rem(lane, PAIR) < head_dim

    def project_queries(frame):
        def step(chunk, carry):
            at = pl.ds(pl.multiple_of(chunk * CHUNK, CHUNK), CHUNK)
            q = jnp.dot(frames[frame], wq[:, at], preferred_element_type=F32)
            q = q * head_dim ** (-0.5)
            queries[frame, 0:block_len, at] = jnp.where(even, q, 0.0).astype(BF16)
            queries[frame, block_len : 2 * block_len, at] = jnp.where(even, 0.0, q).astype(BF16)
            return carry

        lax.fori_loop(0, chunk_count, step, 0)

    for frame in range(EARLY_QUERIES):
        project_queries(frame)

    def project_stills(slot, first, count):
        def step(chunk, carry):
            at = pl.ds(pl.multiple_of(chunk * CHUNK, CHUNK), CHUNK)
            tokens = stills[slot, first * block_len : (first + count) * block_len, :]
            k = jnp.dot(tokens, wk[:, at], preferred_element_type=F32).astype(BF16)
            v = jnp.dot(tokens, wv[:, at], preferred_element_type=F32).astype(BF16)
            for key in range(count):
                part = slice(key * block_len, (key + 1) * block_len)
                block = slot * key_count + first + key
                key_table[block, at, :] = k[part].T
                for pair in range(CHUNK // PAIR):
                    to = pl.multiple_of(chunk * 2 * CHUNK + pair * 2 * PAIR, PAIR)
                    value_table[block, :, pl.ds(to, PAIR)] = v[part, pair * PAIR : (pair + 1) * PAIR]
            return carry

        lax.fori_loop(0, chunk_count, step, 0)

    for load in loads[2:5]:
        load.wait()
    project_stills(1, 0, key_count)
    for key in range(key_count):
        arrival(0, key).wait_recv()
    project_stills(partners[0][1], 0, key_count)

    for load in loads[5:]:
        load.wait()
    pair_lane = lax.broadcasted_iota(jnp.int32, (block_len, PAIR), 1) < head_dim

    def send(frame, other, source):
        return pltpu.make_async_remote_copy(
            src_ref=stage.at[frame, other], dst_ref=out.at[frame, source],
            send_sem=send_sem.at[frame, other], recv_sem=recv_sem.at[frame, source],
            device_id={"tile": other}, device_id_type=pl.DeviceIdType.MESH,
        )

    def partner(step):
        if tiles & (tiles - 1):
            return lax.rem(me + step, tiles)
        other, bit = 0, 1
        while bit < tiles:
            other = other + lax.rem(me // bit + step // bit, 2) * bit
            bit *= 2
        return other

    def keep(frame):
        return pltpu.make_async_copy(stage.at[frame, me], out.at[frame, me], own_sem.at[frame])

    def attend(frame, keys, values, early=False, late=False):
        def score_block(q, slot, at, scores, most):
            s = jnp.dot(q, key_table[keys[slot], at, :], preferred_element_type=F32)
            scores[:, slot * block_len : (slot + 1) * block_len] = s
            for piece in range(block_len // PAIR):
                part = s[:, piece * PAIR : (piece + 1) * PAIR]
                most = part if most is None else jnp.maximum(most, part)
            return most

        def value_block(slot, wide, scores, most, total):
            p = jnp.concatenate(
                [
                    jnp.exp(scores[:, at : at + PAIR] - most).astype(BF16)
                    for at in range(slot * block_len, (slot + 1) * block_len, PAIR)
                ],
                axis=1,
            )
            term = jnp.dot(p, value_table[values[slot], :, wide], preferred_element_type=F32)
            return term if total is None else total + term

        def close(most, pair, top):
            most = jnp.broadcast_to(jnp.max(most, axis=1, keepdims=True), top.shape)
            if late:
                most = jnp.maximum(most, early_max[pair])
            top[...] = most

        def columns(pair, width):
            return pl.ds(pl.multiple_of(pair * width, width), width)

        def load_query(pair):
            return queries[frame, :, columns(pair, PAIR)]

        def step(pair, scores, top, next_pair, next_scores, next_top):
            most, total, next_most = top[...], None, None
            q = load_query(next_pair)
            if late:
                scale = jnp.exp(early_max[pair] - most)
                total = early_total[pair] * jnp.concatenate([scale, scale], axis=1)
            for slot in range(len(keys)):
                next_most = score_block(q, slot, columns(next_pair, PAIR), next_scores, next_most)
                total = value_block(slot, columns(pair, 2 * PAIR), scores, most, total)
            close(next_most, next_pair, next_top)
            if early:
                early_total[pair] = total
                early_max[pair] = most
                return None
            each = total[:, :PAIR] / total[:, PAIR:]
            both = jnp.where(pair_lane, each[:block_len], each[block_len:])
            context[:, columns(pair, PAIR)] = both.astype(BF16)

        most, q = None, load_query(0)
        for slot in range(len(keys)):
            most = score_block(q, slot, columns(0, PAIR), scores_even, most)
        close(most, 0, max_even)

        def two_pairs(index, carry):
            pair = index * 2
            after = jnp.minimum(pair + 2, pair_count - 1)
            step(pair, scores_even, max_even, pair + 1, scores_odd, max_odd)
            step(pair + 1, scores_odd, max_odd, after, scores_even, max_even)
            return carry

        lax.fori_loop(0, pair_count // 2, two_pairs, 0)

    def used(frame, slot):
        return slot < counts[0, frame]

    def named(frame, position):
        keys, values = [], []
        for key in range(key_count):
            there = jnp.int32(0)
            for slot in range(slot_count):
                same = (matches[0, frame, slot] == key * 3 + position) & used(frame, slot)
                there = there + jnp.where(same, 1, 0)
            block = position * key_count + key
            keys.append(jnp.where(there > 0, block, key_count))
            values.append(jnp.where(there > 0, block, 3 * key_count))
        return keys, values

    def finish_frame(frame):
        for chunk in range(chunk_count):
            at = slice(chunk * CHUNK, (chunk + 1) * CHUNK)
            update = jnp.dot(context[...], wo[:, at], preferred_element_type=F32)
            mixed = frames[frame, :, at].astype(F32) + update
            if exchange:
                for other in range(tiles):
                    piece = [
                        mixed[row * col_count + other * cols : row * col_count + (other + 1) * cols]
                        for row in range(rows)
                    ]
                    stage[frame, other, :, at] = jnp.concatenate(piece, axis=0).astype(BF16)
            else:
                stage[frame, 0, :, at] = mixed.astype(BF16)

        if exchange:

            def start(step, carry):
                send(frame, partner(tiles - step), me).start()
                return carry

            lax.fori_loop(1, tiles, start, 0)
            keep(frame).start()
        else:
            pltpu.make_async_copy(stage.at[frame, 0], out.at[frame], own_sem.at[frame]).start()

    def one_frame(frame, carry):
        keys, values = [], []
        for slot in range(slot_count):
            chosen = jnp.where(used(frame, slot), matches[0, frame, slot], matches[0, frame, 0])
            block = lax.rem(chosen, 3) * key_count + lax.div(chosen, 3)
            keys.append(block)
            values.append(jnp.where(used(frame, slot), block, 3 * key_count))
        if EARLY_QUERIES < frame_count:

            @pl.when(frame >= EARLY_QUERIES)
            def _():
                project_queries(frame)

        attend(frame, keys, values)
        finish_frame(frame)
        return carry

    own_keys, own_values = named(0, 1)
    near_keys, near_values = named(0, partners[0][1])
    attend(0, own_keys + near_keys, own_values + near_values, early=True)

    @pl.when(has_far)
    def _():
        for key in range(key_count):
            arrival(1, key).wait_recv()
            project_stills(partners[1][1], key, 1)

    attend(0, *named(0, partners[1][1]), late=True)
    finish_frame(0)
    lax.fori_loop(1, frame_count, one_frame, 0)

    @pl.when(has_far)
    def _():
        for key in range(key_count):
            halo(1, key).wait_send()

    for key in range(key_count):
        halo(0, key).wait_send()

    def finish(frame, carry):
        if exchange:

            def end(step, carry):
                other = lax.rem(me + step, tiles)
                send(frame, other, me).wait_send()
                send(frame, other, other).wait_recv()
                return carry

            lax.fori_loop(1, tiles, end, 0)
            keep(frame).wait()
        else:
            pltpu.make_async_copy(stage.at[frame, 0], out.at[frame], own_sem.at[frame]).wait()
        return carry

    lax.fori_loop(0, frame_count, finish, 0)


def shards(tiles, frames, keyframes, matches, counts, w_query, w_key, w_value, w_out):
    frame_count, row_count, col_count, model_dim = frames.shape
    key_count = keyframes.shape[0]
    block_len = row_count * col_count
    slots = matches.shape[2]
    cols = col_count // tiles
    exchange = cols % 8 == 0
    pieces = tiles if exchange else 1
    piece_len = block_len // pieces
    if exchange:
        out_shape = (frame_count, tiles, piece_len, model_dim)
    else:
        out_shape = (frame_count, block_len, model_dim)
    weight = pltpu.VMEM((model_dim, model_dim), BF16)
    products = (4 * frame_count + 12 * key_count) * block_len * model_dim * model_dim
    products += 4 * frame_count * slots * block_len * block_len * model_dim
    mixed = pl.pallas_call(
        functools.partial(kernel, tiles, exchange, col_count),
        out_shape=jax.ShapeDtypeStruct(out_shape, BF16),
        in_specs=[pl.BlockSpec(memory_space=pl.ANY)] * 8,
        out_specs=pl.BlockSpec(memory_space=pl.ANY),
        scratch_shapes=[
            pltpu.SMEM(matches.shape, jnp.int32),
            pltpu.SMEM(counts.shape, jnp.int32),
            pltpu.VMEM((frame_count, block_len, model_dim), BF16),
            pltpu.VMEM((3, key_count * block_len, model_dim), BF16),
            weight, weight, weight, weight,
            pltpu.VMEM((frame_count, 2 * block_len, model_dim), BF16),
            pltpu.VMEM((3 * key_count, model_dim, block_len), BF16),
            pltpu.VMEM((3 * key_count + 1, block_len, 2 * model_dim), BF16),
            pltpu.VMEM((block_len, model_dim), BF16),
            pltpu.VMEM((frame_count, pieces, piece_len, model_dim), BF16),
            pltpu.VMEM((2 * block_len, slots * block_len), F32),
            pltpu.VMEM((2 * block_len, slots * block_len), F32),
            pltpu.VMEM((2 * block_len, PAIR), F32),
            pltpu.VMEM((2 * block_len, PAIR), F32),
            pltpu.VMEM((HEADS // 2, 2 * block_len, 2 * PAIR), F32),
            pltpu.VMEM((HEADS // 2, 2 * block_len, PAIR), F32),
            pltpu.SemaphoreType.DMA((8,)),
            pltpu.SemaphoreType.DMA((2, key_count)),
            pltpu.SemaphoreType.DMA((2, key_count)),
            pltpu.SemaphoreType.DMA((frame_count, pieces)),
            pltpu.SemaphoreType.DMA((frame_count, pieces)),
            pltpu.SemaphoreType.DMA((frame_count,)),
        ],
        compiler_params=pltpu.CompilerParams(
            collective_id=0, has_side_effects=True, vmem_limit_bytes=60 * 1024 * 1024
        ),
        cost_estimate=pl.CostEstimate(
            flops=products, bytes_accessed=16 * 1024 * 1024,
            transcendentals=frame_count * slots * HEADS * block_len * block_len,
        ),
        name="attend_and_relay",
    )(
        matches, counts,
        frames.reshape(frame_count, block_len, model_dim),
        keyframes.reshape(key_count * block_len, model_dim),
        w_query, w_key, w_value, w_out,
    )
    if exchange:
        return mixed.reshape(frame_count, tiles * row_count, cols, model_dim)
    mixed = mixed.reshape(frame_count, row_count, col_count, model_dim)
    return lax.all_to_all(mixed, "tile", split_axis=2, concat_axis=1, tiled=True)


def solution(mesh):
    placed = (
        P("clip", "tile", None, None),
        P("clip", "tile", None, None),
        P("tile", "clip", None),
        P("tile", "clip"),
        P(),
        P(),
        P(),
        P(),
    )
    return jax.shard_map(
        functools.partial(shards, mesh.shape["tile"]),
        mesh=mesh, in_specs=placed, out_specs=P("clip", None, "tile", None), check_vma=False,
    )
```

profile of v0, /device:TPU:0, one launch (start us, length us, event | category | flops | bytes accessed | tf_op | source)
XLA Modules:
  0.0 80.7 jit_solution(17549253500295344143)
XLA Ops:
  0.0 77.6 %attend_and_relay.1 = bf16[4,16,16,1024]{3,2,1,0:T(8,128)(2,1)} custom-call(s32[1,4,4]{2,1,0:T(4,128)} %matches_in.1, s32[1,4]{1,0:T(1,128)} %counts_in.1, bf16[4,256,1024]{2,1,0:T(8,128)(2,1)} %bitcast.4, bf16[512,1024]{1,0:T(8,128)(2,1)} %bitcast.5, bf16[1024,1024]{1,0:T(8,128)(2,1)} %wq_in.1, bf16[1024,1024]{1,0:T(8,128)(2,1)} %wk_in.1, ...), custom_call_target="tpu_custom_call" | custom-call | flops 15032385536 | bytes 16777216 | tf_op jit(solution)/shard_map/attend_and_relay/pallas_call | solution.py:348
  77.6 3.1 %copy.10 = bf16[4,32,8,1024]{3,2,1,0:T(8,128)(2,1)} copy(bf16[4,32,8,1024]{3,2,1,0:T(8,128)(2,1)} %bitcast.3) | data formatting | bytes 4194304
where the time goes:
time: 80.8 us; the launch traced here: 80.7 us
  Pallas kernels  77.6 us (96%)
  local copies, waits for them, and re-layouts  3.08 us (4%)
    pallas_call x1, Pallas kernels, shards(): pl.pallas_call(functools.partial(kernel, tiles, exchange, col_count), out...  77.6 us
    unnamed x1, local copies, waits for them, and re-layouts  3.08 us

commit v1 on v0

v1 whole, which is shorter than its diff:
```python
import functools

import jax
import jax.numpy as jnp
from jax import lax
from jax.experimental import pallas as pl
from jax.experimental.pallas import tpu as pltpu
from jax.sharding import PartitionSpec as P

HEADS = 16
PAIR = 128
CHUNK = 512
FAST_EARLY = 1
F32 = jnp.float32
BF16 = jnp.bfloat16


def kernel(
    tiles, exchange,
    matches_in, counts_in, frames_in, keys_in, wq_in, wk_in, wv_in, wo_in,
    out,
    matches, counts, frames, stills, wq, wk, wv, wo, queries, key_table, value_table, context,
    stage, scores_even, scores_odd, max_even, max_odd, early_total, early_max,
    load_sem, halo_send, halo_recv, send_sem, recv_sem, own_sem,
):
    _, frame_count, rows, half_cols, model_dim = frames.shape
    piece_len = rows * half_cols
    block_len = 2 * piece_len
    key_count = stills.shape[1] // block_len
    slot_count = matches.shape[2]
    head_dim = model_dim // HEADS
    pair_count = model_dim // PAIR
    chunk_count = model_dim // CHUNK
    half_tiles = tiles // 2
    cols = half_cols // half_tiles
    me = lax.axis_index("tile")
    side = me // half_tiles

    def image_half(half):
        return jnp.where(half == 0, 1 - side, side)

    def half_columns(half):
        return pl.ds(pl.multiple_of(image_half(half) * half_cols, half_cols), half_cols)

    loads = [
        pltpu.make_async_copy(src, dst, load_sem.at[i])
        for i, (src, dst) in enumerate(
            [
                (keys_in, stills.at[1]), (wk_in, wk), (wv_in, wv),
                (frames_in.at[:, :, half_columns(0)], frames.at[0]), (wq_in, wq),
                (frames_in.at[:, :, half_columns(1)], frames.at[1]), (wo_in, wo),
                (matches_in, matches), (counts_in, counts),
            ]
        )
    ]
    for load in loads:
        load.start()

    barrier = pltpu.get_barrier_semaphore()

    def greet(step, carry):
        other = lax.rem(me + step, tiles)
        pl.semaphore_signal(
            barrier, inc=1, device_id={"tile": other}, device_id_type=pl.DeviceIdType.MESH
        )
        return carry

    lax.fori_loop(1, tiles, greet, 0)

    def fill(block, carry):
        one = jnp.where(block < 3 * key_count, 1.0, 0.0).astype(BF16)
        for pair in range(pair_count):
            value_table[block, :, pl.ds(pair * 2 * PAIR + PAIR, PAIR)] = jnp.full(
                (block_len, PAIR), 1.0, F32
            ).astype(BF16) * one
        return carry

    odd = lax.rem(me, 2)
    partners = ((me + 1 - 2 * odd, 2 - 2 * odd), (me - 1 + 2 * odd, 2 * odd))
    far = partners[1][0]
    has_far = (far >= 0) & (far < tiles)
    place = lax.rem(me, 4)
    slow = ((place == 1) | (place == 2)) & (me != 1) & (me != tiles - 2)
    early_count = jnp.where(has_far, jnp.where(slow, frame_count, FAST_EARLY), 0)

    pl.semaphore_wait(barrier, tiles - 1)

    def halo(kind, key):
        part = pl.ds(key * block_len, block_len)
        return pltpu.make_async_remote_copy(
            src_ref=keys_in.at[part], dst_ref=stills.at[partners[1 - kind][1], part],
            send_sem=halo_send.at[kind, key], recv_sem=halo_recv.at[kind, key],
            device_id={"tile": partners[kind][0]}, device_id_type=pl.DeviceIdType.MESH,
        )

    def arrival(kind, key):
        part = pl.ds(key * block_len, block_len)
        return pltpu.make_async_remote_copy(
            src_ref=keys_in.at[part], dst_ref=stills.at[partners[kind][1], part],
            send_sem=halo_send.at[kind, key], recv_sem=halo_recv.at[kind, key],
            device_id={"tile": partners[kind][0]}, device_id_type=pl.DeviceIdType.MESH,
        )

    @pl.when(has_far)
    def _():
        for key in range(key_count):
            halo(1, key).start()

    for key in range(key_count):
        halo(0, key).start()

    lax.fori_loop(0, 3 * key_count + 1, fill, 0)
    for pair in range(pair_count):
        value_table[3 * key_count, :, pl.ds(pair * 2 * PAIR, PAIR)] = jnp.zeros(
            (block_len, PAIR), BF16
        )

    lane = lax.broadcasted_iota(jnp.int32, (piece_len, CHUNK), 1)
    even = lax.rem(lane, PAIR) < head_dim

    def project_queries(half):
        def step(chunk, carry):
            at = pl.ds(pl.multiple_of(chunk * CHUNK, CHUNK), CHUNK)
            tokens = frames[half].reshape(frame_count * piece_len, model_dim)
            q = jnp.dot(tokens, wq[:, at], preferred_element_type=F32)
            q = q * head_dim ** (-0.5)
            for frame in range(frame_count):
                part = q[frame * piece_len : (frame + 1) * piece_len]
                piece = half * frame_count + frame
                queries[piece, 0:piece_len, at] = jnp.where(even, part, 0.0).astype(BF16)
                queries[piece, piece_len : 2 * piece_len, at] = jnp.where(even, 0.0, part).astype(BF16)
            return carry

        lax.fori_loop(0, chunk_count, step, 0)

    def project_stills(slot, first, count):
        def step(chunk, carry):
            at = pl.ds(pl.multiple_of(chunk * CHUNK, CHUNK), CHUNK)
            tokens = stills[slot, first * block_len : (first + count) * block_len, :]
            k = jnp.dot(tokens, wk[:, at], preferred_element_type=F32).astype(BF16)
            v = jnp.dot(tokens, wv[:, at], preferred_element_type=F32).astype(BF16)
            for key in range(count):
                part = slice(key * block_len, (key + 1) * block_len)
                block = slot * key_count + first + key
                key_table[block, at, :] = k[part].T
                for pair in range(CHUNK // PAIR):
                    to = pl.multiple_of(chunk * 2 * CHUNK + pair * 2 * PAIR, PAIR)
                    value_table[block, :, pl.ds(to, PAIR)] = v[part, pair * PAIR : (pair + 1) * PAIR]
            return carry

        lax.fori_loop(0, chunk_count, step, 0)

    for load in loads[:3]:
        load.wait()
    project_stills(1, 0, key_count)
    for load in loads[3:]:
        load.wait()

    def project_half(half, carry):
        project_queries(half)
        return carry

    lax.fori_loop(0, jnp.where(slow, 2, 1), project_half, 0)
    for key in range(key_count):
        arrival(0, key).wait_recv()
    project_stills(partners[0][1], 0, key_count)
    pair_lane = lax.broadcasted_iota(jnp.int32, (piece_len, PAIR), 1) < head_dim

    def send(frame, other, source):
        return pltpu.make_async_remote_copy(
            src_ref=stage.at[frame, other], dst_ref=out.at[frame, source],
            send_sem=send_sem.at[frame, other], recv_sem=recv_sem.at[frame, source],
            device_id={"tile": other}, device_id_type=pl.DeviceIdType.MESH,
        )

    def keep(frame):
        return pltpu.make_async_copy(stage.at[frame, me], out.at[frame, me], own_sem.at[0, frame])

    def place_half(frame, half):
        return pltpu.make_async_copy(
            stage.at[frame, image_half(half)], out.at[frame, :, half_columns(half)],
            own_sem.at[half, frame],
        )

    def attend(piece, keys, values, early=False, late=False):
        def score_block(q, slot, at, scores, most):
            s = jnp.dot(q, key_table[keys[slot], at, :], preferred_element_type=F32)
            scores[:, slot * block_len : (slot + 1) * block_len] = s
            for part in range(block_len // PAIR):
                some = s[:, part * PAIR : (part + 1) * PAIR]
                most = some if most is None else jnp.maximum(most, some)
            return most

        def value_block(slot, wide, scores, most, total):
            p = jnp.concatenate(
                [
                    jnp.exp(scores[:, at : at + PAIR] - most).astype(BF16)
                    for at in range(slot * block_len, (slot + 1) * block_len, PAIR)
                ],
                axis=1,
            )
            term = jnp.dot(p, value_table[values[slot], :, wide], preferred_element_type=F32)
            return term if total is None else total + term

        def close(most, pair, top):
            most = jnp.broadcast_to(jnp.max(most, axis=1, keepdims=True), top.shape)
            if late:
                most = jnp.maximum(most, early_max[piece, pair])
            top[...] = most

        def columns(pair, width):
            return pl.ds(pl.multiple_of(pair * width, width), width)

        def load_query(pair):
            return queries[piece, :, columns(pair, PAIR)]

        def step(pair, scores, top, next_pair, next_scores, next_top):
            most, total, next_most = top[...], None, None
            q = load_query(next_pair)
            if late:
                scale = jnp.exp(early_max[piece, pair] - most)
                total = early_total[piece, pair] * jnp.concatenate([scale, scale], axis=1)
            for slot in range(len(keys)):
                next_most = score_block(q, slot, columns(next_pair, PAIR), next_scores, next_most)
                total = value_block(slot, columns(pair, 2 * PAIR), scores, most, total)
            close(next_most, next_pair, next_top)
            if early:
                early_total[piece, pair] = total
                early_max[piece, pair] = most
                return None
            each = total[:, :PAIR] / total[:, PAIR:]
            both = jnp.where(pair_lane, each[:piece_len], each[piece_len:])
            context[:, columns(pair, PAIR)] = both.astype(BF16)

        most, q = None, load_query(0)
        for slot in range(len(keys)):
            most = score_block(q, slot, columns(0, PAIR), scores_even, most)
        close(most, 0, max_even)

        def two_pairs(index, carry):
            pair = index * 2
            after = jnp.minimum(pair + 2, pair_count - 1)
            step(pair, scores_even, max_even, pair + 1, scores_odd, max_odd)
            step(pair + 1, scores_odd, max_odd, after, scores_even, max_even)
            return carry

        lax.fori_loop(0, pair_count // 2, two_pairs, 0)

    def used(frame, slot):
        return slot < counts[0, frame]

    def named(frame, position):
        keys, values = [], []
        for key in range(key_count):
            there = jnp.int32(0)
            for slot in range(slot_count):
                same = (matches[0, frame, slot] == key * 3 + position) & used(frame, slot)
                there = there + jnp.where(same, 1, 0)
            block = position * key_count + key
            keys.append(jnp.where(there > 0, block, key_count))
            values.append(jnp.where(there > 0, block, 3 * key_count))
        return keys, values

    def partner(half, step):
        top = lax.rem(me // half_tiles, 2)
        other, bit = jnp.where(half == 0, 1 - top, top) * half_tiles, 1
        while bit < half_tiles:
            mine = lax.rem(me // bit, 2)
            other = other + (1 - mine if step // bit % 2 else mine) * bit
            bit *= 2
        return other

    def finish_piece(half, frame):
        for chunk in range(chunk_count):
            at = slice(chunk * CHUNK, (chunk + 1) * CHUNK)
            update = jnp.dot(context[...], wo[:, at], preferred_element_type=F32)
            mixed = frames[half, frame, :, :, at].reshape(piece_len, CHUNK).astype(F32) + update
            if exchange:
                first = image_half(half) * half_tiles
                for other in range(half_tiles):
                    group = [
                        mixed[row * half_cols + other * cols : row * half_cols + (other + 1) * cols]
                        for row in range(rows)
                    ]
                    stage[frame, first + other, :, at] = jnp.concatenate(group, axis=0).astype(BF16)
            else:
                stage[frame, image_half(half), :, :, at] = mixed.reshape(rows, half_cols, CHUNK).astype(BF16)

        if exchange:
            order = sorted(range(half_tiles), key=lambda step: (step // 2 % 2, -step))
            for step in order:
                other = partner(half, step)
                if step:
                    send(frame, other, me).start()
                    continue

                @pl.when(half == 0)
                def _():
                    send(frame, other, me).start()

                @pl.when(half != 0)
                def _():
                    keep(frame).start()
        else:
            place_half(frame, half).start()

    def one_piece(piece, carry):
        half = piece // frame_count
        frame = lax.rem(piece, frame_count)
        keys, values = [], []
        for slot in range(slot_count):
            chosen = jnp.where(used(frame, slot), matches[0, frame, slot], matches[0, frame, 0])
            block = lax.rem(chosen, 3) * key_count + lax.div(chosen, 3)
            keys.append(block)
            values.append(jnp.where(used(frame, slot), block, 3 * key_count))

        @pl.when((piece == frame_count) & jnp.logical_not(slow))
        def _():
            project_queries(1)

        attend(piece, keys, values)
        finish_piece(half, frame)
        return carry

    def early_piece(piece, carry):
        own_keys, own_values = named(piece, 1)
        near_keys, near_values = named(piece, partners[0][1])
        attend(piece, own_keys + near_keys, own_values + near_values, early=True)
        return carry

    def late_piece(piece, carry):
        attend(piece, *named(piece, partners[1][1]), late=True)
        finish_piece(jnp.int32(0), piece)
        return carry

    lax.fori_loop(0, early_count, early_piece, 0)

    @pl.when(has_far)
    def _():
        for key in range(key_count):
            arrival(1, key).wait_recv()
            project_stills(partners[1][1], key, 1)

    lax.fori_loop(0, early_count, late_piece, 0)
    lax.fori_loop(early_count, 2 * frame_count, one_piece, 0)

    @pl.when(has_far)
    def _():
        for key in range(key_count):
            halo(1, key).wait_send()

    for key in range(key_count):
        halo(0, key).wait_send()

    def finish(frame, carry):
        if exchange:

            def end(step, carry):
                other = lax.rem(me + step, tiles)
                send(frame, other, me).wait_send()
                send(frame, other, other).wait_recv()
                return carry

            lax.fori_loop(1, tiles, end, 0)
            keep(frame).wait()
        else:
            for half in range(2):
                place_half(frame, half).wait()
        return carry

    lax.fori_loop(0, frame_count, finish, 0)


def shards(tiles, frames, keyframes, matches, counts, w_query, w_key, w_value, w_out):
    frame_count, row_count, col_count, model_dim = frames.shape
    key_count = keyframes.shape[0]
    block_len = row_count * col_count
    half_cols = col_count // 2
    piece_len = row_count * half_cols
    slots = matches.shape[2]
    cols = col_count // tiles
    exchange = cols % 8 == 0 and tiles & (tiles - 1) == 0
    if exchange:
        out_shape = (frame_count, tiles, row_count * cols, model_dim)
        stage_shape = out_shape
    else:
        out_shape = (frame_count, row_count, col_count, model_dim)
        stage_shape = (frame_count, 2, row_count, half_cols, model_dim)
    weight = pltpu.VMEM((model_dim, model_dim), BF16)
    products = (4 * frame_count + 12 * key_count) * block_len * model_dim * model_dim
    products += 4 * frame_count * slots * block_len * block_len * model_dim
    mixed = pl.pallas_call(
        functools.partial(kernel, tiles, exchange),
        out_shape=jax.ShapeDtypeStruct(out_shape, BF16),
        in_specs=[pl.BlockSpec(memory_space=pl.ANY)] * 8,
        out_specs=pl.BlockSpec(memory_space=pl.ANY),
        scratch_shapes=[
            pltpu.SMEM(matches.shape, jnp.int32),
            pltpu.SMEM(counts.shape, jnp.int32),
            pltpu.VMEM((2, frame_count, row_count, half_cols, model_dim), BF16),
            pltpu.VMEM((3, key_count * block_len, model_dim), BF16),
            weight, weight, weight, weight,
            pltpu.VMEM((2 * frame_count, 2 * piece_len, model_dim), BF16),
            pltpu.VMEM((3 * key_count, model_dim, block_len), BF16),
            pltpu.VMEM((3 * key_count + 1, block_len, 2 * model_dim), BF16),
            pltpu.VMEM((piece_len, model_dim), BF16),
            pltpu.VMEM(stage_shape, BF16),
            pltpu.VMEM((2 * piece_len, slots * block_len), F32),
            pltpu.VMEM((2 * piece_len, slots * block_len), F32),
            pltpu.VMEM((2 * piece_len, PAIR), F32),
            pltpu.VMEM((2 * piece_len, PAIR), F32),
            pltpu.VMEM((frame_count, HEADS // 2, 2 * piece_len, 2 * PAIR), F32),
            pltpu.VMEM((frame_count, HEADS // 2, 2 * piece_len, PAIR), F32),
            pltpu.SemaphoreType.DMA((9,)),
            pltpu.SemaphoreType.DMA((2, key_count)),
            pltpu.SemaphoreType.DMA((2, key_count)),
            pltpu.SemaphoreType.DMA((frame_count, tiles)),
            pltpu.SemaphoreType.DMA((frame_count, tiles)),
            pltpu.SemaphoreType.DMA((2, frame_count)),
        ],
        compiler_params=pltpu.CompilerParams(
            collective_id=0, has_side_effects=True, vmem_limit_bytes=60 * 1024 * 1024
        ),
        cost_estimate=pl.CostEstimate(
            flops=products, bytes_accessed=16 * 1024 * 1024,
            transcendentals=frame_count * slots * HEADS * block_len * block_len,
        ),
        name="attend_and_relay",
    )(
        matches, counts, frames,
        keyframes.reshape(key_count * block_len, model_dim),
        w_query, w_key, w_value, w_out,
    )
    if exchange:
        return mixed.reshape(frame_count, tiles * row_count, cols, model_dim)
    return lax.all_to_all(mixed, "tile", split_axis=2, concat_axis=1, tiled=True)


def solution(mesh):
    placed = (
        P("clip", "tile", None, None),
        P("clip", "tile", None, None),
        P("tile", "clip", None),
        P("tile", "clip"),
        P(),
        P(),
        P(),
        P(),
    )
    return jax.shard_map(
        functools.partial(shards, mesh.shape["tile"]),
        mesh=mesh, in_specs=placed, out_specs=P("clip", None, "tile", None), check_vma=False,
    )
```

time: 80.8 us -> 75 us (0.928)
  the two profiles are of different devices: /device:TPU:0 before, /device:TPU:5 now
where the time goes in v1:
time: 75 us; the launch traced here: 74.8 us
  Pallas kernels  71.7 us (96%)
  local copies, waits for them, and re-layouts  3.08 us (4%)
    pallas_call x1, Pallas kernels, shards(): pl.pallas_call(functools.partial(kernel, tiles, exchange), out_shape=jax....  71.7 us
    unnamed x1, local copies, waits for them, and re-layouts  3.08 us

profile of v1, /device:TPU:5, one launch (start us, length us, event | category | flops | bytes accessed | tf_op | source)
XLA Modules:
  0.0 74.8 jit_solution(16270438022408102222)
XLA Ops:
  0.0 71.7 %attend_and_relay.1 = bf16[4,16,16,1024]{3,2,1,0:T(8,128)(2,1)} custom-call(s32[1,4,4]{2,1,0:T(4,128)} %matches_in.1, s32[1,4]{1,0:T(1,128)} %counts_in.1, bf16[4,2,128,1024]{3,2,1,0:T(8,128)(2,1)} %frames_in.1, bf16[512,1024]{1,0:T(8,128)(2,1)} %bitcast.3, bf16[1024,1024]{1,0:T(8,128)(2,1)} %wq_in.1, bf16[1024,1024]{1,0:T(8,128)(2,1)} %wk_in.1, ...), custom_call_target="tpu_custom_call" | custom-call | flops 15032385536 | bytes 16777216 | tf_op jit(solution)/shard_map/attend_and_relay/pallas_call | solution.py:392
  71.8 3.1 %copy.10 = bf16[4,32,8,1024]{3,2,1,0:T(8,128)(2,1)} copy(bf16[4,32,8,1024]{3,2,1,0:T(8,128)(2,1)} %bitcast.2) | data formatting | bytes 4194304

commit v2 on v1

--- a/solution.py
+++ b/solution.py
@@ -11,6 +11,7 @@
 PAIR = 128
 CHUNK = 512
 FAST_EARLY = 1
+GROUP = 8
 F32 = jnp.float32
 BF16 = jnp.bfloat16
 
@@ -21,7 +22,7 @@
     out,
     matches, counts, frames, stills, wq, wk, wv, wo, queries, key_table, value_table, context,
     stage, scores_even, scores_odd, max_even, max_odd, early_total, early_max,
-    load_sem, halo_send, halo_recv, send_sem, recv_sem, own_sem,
+    load_sem, halo_send, halo_recv, near_send, near_recv, send_sem, recv_sem, own_sem,
 ):
     _, frame_count, rows, half_cols, model_dim = frames.shape
     piece_len = rows * half_cols
@@ -46,7 +47,7 @@
         pltpu.make_async_copy(src, dst, load_sem.at[i])
         for i, (src, dst) in enumerate(
             [
-                (keys_in, stills.at[1]), (wk_in, wk), (wv_in, wv),
+                (keys_in, stills.at[0]), (wk_in, wk), (wv_in, wv),
                 (frames_in.at[:, :, half_columns(0)], frames.at[0]), (wq_in, wq),
                 (frames_in.at[:, :, half_columns(1)], frames.at[1]), (wo_in, wo),
                 (matches_in, matches), (counts_in, counts),
@@ -67,53 +68,66 @@
 
     lax.fori_loop(1, tiles, greet, 0)
 
-    def fill(block, carry):
+    def fill(block):
         one = jnp.where(block < 3 * key_count, 1.0, 0.0).astype(BF16)
         for pair in range(pair_count):
             value_table[block, :, pl.ds(pair * 2 * PAIR + PAIR, PAIR)] = jnp.full(
                 (block_len, PAIR), 1.0, F32
             ).astype(BF16) * one
-        return carry
 
     odd = lax.rem(me, 2)
     partners = ((me + 1 - 2 * odd, 2 - 2 * odd), (me - 1 + 2 * odd, 2 * odd))
     far = partners[1][0]
     has_far = (far >= 0) & (far < tiles)
     place = lax.rem(me, 4)
-    slow = ((place == 1) | (place == 2)) & (me != 1) & (me != tiles - 2)
+    inner = (place == 1) | (place == 2)
+    slow = inner & (me != 1) & (me != tiles - 2)
+    held = has_far & inner & (far != 1) & (far != tiles - 2)
     early_count = jnp.where(has_far, jnp.where(slow, frame_count, FAST_EARLY), 0)
 
-    pl.semaphore_wait(barrier, tiles - 1)
-
-    def halo(kind, key):
-        part = pl.ds(key * block_len, block_len)
-        return pltpu.make_async_remote_copy(
-            src_ref=keys_in.at[part], dst_ref=stills.at[partners[1 - kind][1], part],
-            send_sem=halo_send.at[kind, key], recv_sem=halo_recv.at[kind, key],
-            device_id={"tile": partners[kind][0]}, device_id_type=pl.DeviceIdType.MESH,
-        )
-
-    def arrival(kind, key):
-        part = pl.ds(key * block_len, block_len)
-        return pltpu.make_async_remote_copy(
-            src_ref=keys_in.at[part], dst_ref=stills.at[partners[kind][1], part],
-            send_sem=halo_send.at[kind, key], recv_sem=halo_recv.at[kind, key],
-            device_id={"tile": partners[kind][0]}, device_id_type=pl.DeviceIdType.MESH,
-        )
-
-    @pl.when(has_far)
-    def _():
-        for key in range(key_count):
-            halo(1, key).start()
-
     for key in range(key_count):
-        halo(0, key).start()
-
-    lax.fori_loop(0, 3 * key_count + 1, fill, 0)
+        fill(key_count + key)
+        fill(partners[1][1] * key_count + key)
+    fill(3 * key_count)
     for pair in range(pair_count):
         value_table[3 * key_count, :, pl.ds(pair * 2 * PAIR, PAIR)] = jnp.zeros(
             (block_len, PAIR), BF16
         )
+    pl.semaphore_wait(barrier, tiles - 1)
+
+    def halo(key):
+        part = pl.ds(key * block_len, block_len)
+        return pltpu.make_async_remote_copy(
+            src_ref=keys_in.at[part], dst_ref=stills.at[1, part],
+            send_sem=halo_send.at[key], recv_sem=halo_recv.at[key],
+            device_id={"tile": far}, device_id_type=pl.DeviceIdType.MESH,
+        )
+
+    def start_halo():
+        for key in range(key_count):
+            halo(key).start()
+
+    def shared(key, chunk, position):
+        block = position * key_count + key
+        own = key_count + key
+        narrow = pl.ds(pl.multiple_of(chunk * CHUNK, CHUNK), CHUNK)
+        wide = pl.ds(pl.multiple_of(chunk * 2 * CHUNK, 2 * CHUNK), 2 * CHUNK)
+        pieces = (
+            (key_table.at[own, narrow], key_table.at[block, narrow]),
+            (value_table.at[own, :, wide], value_table.at[block, :, wide]),
+        )
+        return [
+            pltpu.make_async_remote_copy(
+                src_ref=src, dst_ref=dst,
+                send_sem=near_send.at[kind, key, chunk], recv_sem=near_recv.at[kind, key, chunk],
+                device_id={"tile": partners[0][0]}, device_id_type=pl.DeviceIdType.MESH,
+            )
+            for kind, (src, dst) in enumerate(pieces)
+        ]
+
+    @pl.when(has_far & jnp.logical_not(held))
+    def _():
+        start_halo()
 
     lane = lax.broadcasted_iota(jnp.int32, (piece_len, CHUNK), 1)
     even = lax.rem(lane, PAIR) < head_dim
@@ -133,10 +147,10 @@
 
         lax.fori_loop(0, chunk_count, step, 0)
 
-    def project_stills(slot, first, count):
+    def project_stills(source, slot, first, count, share=False):
         def step(chunk, carry):
             at = pl.ds(pl.multiple_of(chunk * CHUNK, CHUNK), CHUNK)
-            tokens = stills[slot, first * block_len : (first + count) * block_len, :]
+            tokens = stills[source, first * block_len : (first + count) * block_len, :]
             k = jnp.dot(tokens, wk[:, at], preferred_element_type=F32).astype(BF16)
             v = jnp.dot(tokens, wv[:, at], preferred_element_type=F32).astype(BF16)
             for key in range(count):
@@ -146,13 +160,16 @@
                 for pair in range(CHUNK // PAIR):
                     to = pl.multiple_of(chunk * 2 * CHUNK + pair * 2 * PAIR, PAIR)
                     value_table[block, :, pl.ds(to, PAIR)] = v[part, pair * PAIR : (pair + 1) * PAIR]
+                if share:
+                    for copy in shared(key, chunk, partners[1][1]):
+                        copy.start()
             return carry
 
         lax.fori_loop(0, chunk_count, step, 0)
 
     for load in loads[:3]:
         load.wait()
-    project_stills(1, 0, key_count)
+    project_stills(0, 1, 0, key_count, share=True)
     for load in loads[3:]:
         load.wait()
 
@@ -162,8 +179,9 @@
 
     lax.fori_loop(0, jnp.where(slow, 2, 1), project_half, 0)
     for key in range(key_count):
-        arrival(0, key).wait_recv()
-    project_stills(partners[0][1], 0, key_count)
+        for chunk in range(chunk_count):
+            for copy in shared(key, chunk, partners[0][1]):
+                copy.wait_recv()
     pair_lane = lax.broadcasted_iota(jnp.int32, (piece_len, PAIR), 1) < head_dim
 
     def send(frame, other, source):
@@ -237,14 +255,15 @@
             most = score_block(q, slot, columns(0, PAIR), scores_even, most)
         close(most, 0, max_even)
 
-        def two_pairs(index, carry):
-            pair = index * 2
-            after = jnp.minimum(pair + 2, pair_count - 1)
-            step(pair, scores_even, max_even, pair + 1, scores_odd, max_odd)
-            step(pair + 1, scores_odd, max_odd, after, scores_even, max_even)
+        def group(index, carry):
+            for inner_pair in range(0, GROUP, 2):
+                pair = index * GROUP + inner_pair
+                after = jnp.minimum(pair + 2, pair_count - 1)
+                step(pair, scores_even, max_even, pair + 1, scores_odd, max_odd)
+                step(pair + 1, scores_odd, max_odd, after, scores_even, max_even)
             return carry
 
-        lax.fori_loop(0, pair_count // 2, two_pairs, 0)
+        lax.fori_loop(0, pair_count // GROUP, group, 0)
 
     def used(frame, slot):
         return slot < counts[0, frame]
@@ -314,7 +333,7 @@
             keys.append(block)
             values.append(jnp.where(used(frame, slot), block, 3 * key_count))
 
-        @pl.when((piece == frame_count) & jnp.logical_not(slow))
+        @pl.when((piece == frame_count) & jnp.logical_not(has_far))
         def _():
             project_queries(1)
 
@@ -326,6 +345,11 @@
         own_keys, own_values = named(piece, 1)
         near_keys, near_values = named(piece, partners[0][1])
         attend(piece, own_keys + near_keys, own_values + near_values, early=True)
+
+        @pl.when((piece == 0) & held)
+        def _():
+            start_halo()
+
         return carry
 
     def late_piece(piece, carry):
@@ -338,8 +362,13 @@
     @pl.when(has_far)
     def _():
         for key in range(key_count):
-            arrival(1, key).wait_recv()
-            project_stills(partners[1][1], key, 1)
+            halo(key).wait_recv()
+            project_stills(1, partners[1][1], key, 1)
+            if key == 0:
+
+                @pl.when(jnp.logical_not(slow))
+                def _():
+                    project_queries(1)
 
     lax.fori_loop(0, early_count, late_piece, 0)
     lax.fori_loop(early_count, 2 * frame_count, one_piece, 0)
@@ -347,10 +376,12 @@
     @pl.when(has_far)
     def _():
         for key in range(key_count):
-            halo(1, key).wait_send()
+            halo(key).wait_send()
 
     for key in range(key_count):
-        halo(0, key).wait_send()
+        for chunk in range(chunk_count):
+            for copy in shared(key, chunk, partners[1][1]):
+                copy.wait_send()
 
     def finish(frame, carry):
         if exchange:
@@ -369,6 +400,27 @@
         return carry
 
     lax.fori_loop(0, frame_count, finish, 0)
+
+
+def settle(src, out, held, in_sem, out_sem):
+    frame_count, parts = in_sem.shape
+    step = src.shape[1] // parts
+    places = [(frame, pl.ds(part * step, step)) for frame in range(frame_count) for part in range(parts)]
+    fetch = [
+        pltpu.make_async_copy(src.at[at], held.at[at], in_sem.at[i // parts, i % parts])
+        for i, at in enumerate(places)
+    ]
+    place = [
+        pltpu.make_async_copy(held.at[at], out.at[at], out_sem.at[i // parts, i % parts])
+        for i, at in enumerate(places)
+    ]
+    for copy in fetch:
+        copy.start()
+    for copy, back in zip(fetch, place):
+        copy.wait()
+        back.start()
+    for back in place:
+        back.wait()
 
 
 def shards(tiles, frames, keyframes, matches, counts, w_query, w_key, w_value, w_out):
@@ -398,7 +450,7 @@
             pltpu.SMEM(matches.shape, jnp.int32),
             pltpu.SMEM(counts.shape, jnp.int32),
             pltpu.VMEM((2, frame_count, row_count, half_cols, model_dim), BF16),
-            pltpu.VMEM((3, key_count * block_len, model_dim), BF16),
+            pltpu.VMEM((2, key_count * block_len, model_dim), BF16),
             weight, weight, weight, weight,
             pltpu.VMEM((2 * frame_count, 2 * piece_len, model_dim), BF16),
             pltpu.VMEM((3 * key_count, model_dim, block_len), BF16),
@@ -412,8 +464,10 @@
             pltpu.VMEM((frame_count, HEADS // 2, 2 * piece_len, 2 * PAIR), F32),
             pltpu.VMEM((frame_count, HEADS // 2, 2 * piece_len, PAIR), F32),
             pltpu.SemaphoreType.DMA((9,)),
-            pltpu.SemaphoreType.DMA((2, key_count)),
-            pltpu.SemaphoreType.DMA((2, key_count)),
+            pltpu.SemaphoreType.DMA((key_count,)),
+            pltpu.SemaphoreType.DMA((key_count,)),
+            pltpu.SemaphoreType.DMA((2, key_count, model_dim // CHUNK)),
+            pltpu.SemaphoreType.DMA((2, key_count, model_dim // CHUNK)),
             pltpu.SemaphoreType.DMA((frame_count, tiles)),
             pltpu.SemaphoreType.DMA((frame_count, tiles)),
             pltpu.SemaphoreType.DMA((2, frame_count)),
@@ -432,6 +486,18 @@
         w_query, w_key, w_value, w_out,
     )
     if exchange:
+        mixed = pl.pallas_call(
+            settle,
+            out_shape=jax.ShapeDtypeStruct(out_shape, BF16),
+            in_specs=[pl.BlockSpec(memory_space=pl.ANY)],
+            out_specs=pl.BlockSpec(memory_space=pl.ANY),
+            scratch_shapes=[
+                pltpu.VMEM(out_shape, BF16),
+                pltpu.SemaphoreType.DMA((frame_count, 2)),
+                pltpu.SemaphoreType.DMA((frame_count, 2)),
+            ],
+            name="settle",
+        )(mixed)
         return mixed.reshape(frame_count, tiles * row_count, cols, model_dim)
     return lax.all_to_all(mixed, "tile", split_axis=2, concat_axis=1, tiled=True)
 

time: 75 us -> 73.3 us (0.977)
  local copies, waits for them, and re-layouts: 3.08 us -> 0 us
  Pallas kernels: 71.7 us -> 73.2 us
    unnamed x1 -> x0, local copies, waits for them, and re-layouts: 3.08 us -> none
    pallas_call x0 -> x1, Pallas kernels: none -> 2.39 us  [shards(): pl.pallas_call(settle, out_shape=jax.ShapeDtypeStruct(out_shape, BF16), i...]
    pallas_call x1, Pallas kernels: 71.7 us -> 70.8 us  [shards(): pl.pallas_call(functools.partial(kernel, tiles, exchange), out_shape=jax....]
where the time goes in v2:
time: 73.3 us; the launch traced here: 73.2 us
  Pallas kernels  73.2 us (100%)
    pallas_call x1, Pallas kernels, shards(): pl.pallas_call(functools.partial(kernel, tiles, exchange), out_shape=jax....  70.8 us
    pallas_call x1, Pallas kernels, shards(): pl.pallas_call(settle, out_shape=jax.ShapeDtypeStruct(out_shape, BF16), i...  2.39 us

profile of v2, /device:TPU:5, one launch (start us, length us, event | category | flops | bytes accessed | tf_op | source)
XLA Modules:
  0.0 73.2 jit_solution(550588096425620377)
XLA Ops:
  0.0 70.8 %attend_and_relay.1.src = bf16[4,16,16,1024]{3,2,1,0:T(8,128)(2,1)} custom-call(s32[1,4,4]{2,1,0:T(4,128)} %matches_in.1, s32[1,4]{1,0:T(1,128)} %counts_in.1, bf16[4,2,128,1024]{3,2,1,0:T(8,128)(2,1)} %frames_in.1, bf16[512,1024]{1,0:T(8,128)(2,1)} %bitcast.2, bf16[1024,1024]{1,0:T(8,128)(2,1)} %wq_in.1, bf16[1024,1024]{1,0:T(8,128)(2,1)} %wk_in.1, ...), custom_call_target="tpu_custom_call" | custom-call | flops 15032385536 | bytes 16777216 | tf_op jit(solution)/shard_map/attend_and_relay/pallas_call | solution.py:444
  70.8 2.4 %settle.1 = bf16[4,16,16,1024]{3,2,1,0:T(8,128)(2,1)} custom-call(bf16[4,16,16,1024]{3,2,1,0:T(8,128)(2,1)} %attend_and_relay.1.src), custom_call_target="tpu_custom_call" | custom-call | tf_op jit(solution)/shard_map/settle/pallas_call | solution.py:489

commit v3 on v2

--- a/solution.py
+++ b/solution.py
@@ -12,6 +12,7 @@
 CHUNK = 512
 FAST_EARLY = 1
 GROUP = 8
+RELAYED = 2
 F32 = jnp.float32
 BF16 = jnp.bfloat16
 
@@ -21,8 +22,8 @@
     matches_in, counts_in, frames_in, keys_in, wq_in, wk_in, wv_in, wo_in,
     out,
     matches, counts, frames, stills, wq, wk, wv, wo, queries, key_table, value_table, context,
-    stage, scores_even, scores_odd, max_even, max_odd, early_total, early_max,
-    load_sem, halo_send, halo_recv, near_send, near_recv, send_sem, recv_sem, own_sem,
+    stage, relay, scores_even, scores_odd, max_even, max_odd, early_total, early_max,
+    load_sem, halo_send, halo_recv, near_send, near_recv, relay_recv, relay_send, send_sem, recv_sem, own_sem,
 ):
     _, frame_count, rows, half_cols, model_dim = frames.shape
     piece_len = rows * half_cols
@@ -33,6 +34,7 @@
     pair_count = model_dim // PAIR
     chunk_count = model_dim // CHUNK
     half_tiles = tiles // 2
+    relay_count = relay.shape[0] if exchange and tiles == 16 else 0
     cols = half_cols // half_tiles
     me = lax.axis_index("tile")
     side = me // half_tiles
@@ -280,14 +282,37 @@
             values.append(jnp.where(there > 0, block, 3 * key_count))
         return keys, values
 
-    def partner(half, step):
-        top = lax.rem(me // half_tiles, 2)
+    def partner(half, step, source=me):
+        top = lax.rem(source // half_tiles, 2)
         other, bit = jnp.where(half == 0, 1 - top, top) * half_tiles, 1
         while bit < half_tiles:
-            mine = lax.rem(me // bit, 2)
+            mine = lax.rem(source // bit, 2)
             other = other + (1 - mine if step // bit % 2 else mine) * bit
             bit *= 2
         return other
+
+    across = me + 2 - 4 * lax.rem(me // 2, 2)
+    relayed = (me == 3) | (me == tiles - 4)
+    relays = (me == 1) | (me == tiles - 2)
+
+    def relay_slot(step):
+        return step // 4 * 2 + step % 2
+
+    def hand_over(frame, step, other):
+        return pltpu.make_async_remote_copy(
+            src_ref=stage.at[frame, other], dst_ref=relay.at[frame, relay_slot(step)],
+            send_sem=send_sem.at[frame, other], recv_sem=relay_recv.at[frame, relay_slot(step)],
+            device_id={"tile": across}, device_id_type=pl.DeviceIdType.MESH,
+        )
+
+    def pass_on(frame, step):
+        return pltpu.make_async_remote_copy(
+            src_ref=relay.at[frame, relay_slot(step)], dst_ref=out.at[frame, across],
+            send_sem=relay_send.at[frame, relay_slot(step)], recv_sem=recv_sem.at[frame, across],
+            device_id={"tile": partner(0, step, across)}, device_id_type=pl.DeviceIdType.MESH,
+        )
+
+    relay_steps = [step for step in range(half_tiles) if step // 2 % 2]
 
     def finish_piece(half, frame):
         for chunk in range(chunk_count):
@@ -309,6 +334,18 @@
             order = sorted(range(half_tiles), key=lambda step: (step // 2 % 2, -step))
             for step in order:
                 other = partner(half, step)
+                if step in relay_steps and relay_count:
+                    detour = relayed & (half == 0) & (frame < relay_count)
+
+                    @pl.when(detour)
+                    def _():
+                        hand_over(frame, step, other).start()
+
+                    @pl.when(jnp.logical_not(detour))
+                    def _():
+                        send(frame, other, me).start()
+
+                    continue
                 if step:
                     send(frame, other, me).start()
                     continue
@@ -339,6 +376,14 @@
 
         attend(piece, keys, values)
         finish_piece(half, frame)
+        if relay_count:
+
+            @pl.when(relays & (piece >= 1) & (piece <= relay_count))
+            def _():
+                for step in relay_steps:
+                    hand_over(piece - 1, step, me).wait_recv()
+                    pass_on(piece - 1, step).start()
+
         return carry
 
     def early_piece(piece, carry):
@@ -382,6 +427,14 @@
         for chunk in range(chunk_count):
             for copy in shared(key, chunk, partners[1][1]):
                 copy.wait_send()
+
+    if relay_count:
+
+        @pl.when(relays)
+        def _():
+            for frame in range(relay_count):
+                for step in relay_steps:
+                    pass_on(frame, step).wait_send()
 
     def finish(frame, carry):
         if exchange:
@@ -457,6 +510,7 @@
             pltpu.VMEM((3 * key_count + 1, block_len, 2 * model_dim), BF16),
             pltpu.VMEM((piece_len, model_dim), BF16),
             pltpu.VMEM(stage_shape, BF16),
+            pltpu.VMEM((min(RELAYED, frame_count), 4) + stage_shape[2:], BF16),
             pltpu.VMEM((2 * piece_len, slots * block_len), F32),
             pltpu.VMEM((2 * piece_len, slots * block_len), F32),
             pltpu.VMEM((2 * piece_len, PAIR), F32),
@@ -468,6 +522,8 @@
             pltpu.SemaphoreType.DMA((key_count,)),
             pltpu.SemaphoreType.DMA((2, key_count, model_dim // CHUNK)),
             pltpu.SemaphoreType.DMA((2, key_count, model_dim // CHUNK)),
+            pltpu.SemaphoreType.DMA((min(RELAYED, frame_count), 4)),
+            pltpu.SemaphoreType.DMA((min(RELAYED, frame_count), 4)),
             pltpu.SemaphoreType.DMA((frame_count, tiles)),
             pltpu.SemaphoreType.DMA((frame_count, tiles)),
             pltpu.SemaphoreType.DMA((2, frame_count)),

time: 73.3 us -> 72.1 us (0.984); the launches traced: 73.2 us -> 70.8 us
  Pallas kernels: 73.2 us -> 70.6 us
    pallas_call x1, Pallas kernels: 70.8 us -> 68.2 us  [shards(): pl.pallas_call(functools.partial(kernel, tiles, exchange), out_shape=jax....]
where the time goes in v3:
time: 72.1 us; the launch traced here: 70.8 us
  Pallas kernels  70.6 us (98%)
    pallas_call x1, Pallas kernels, shards(): pl.pallas_call(functools.partial(kernel, tiles, exchange), out_shape=jax....  68.2 us
    pallas_call x1, Pallas kernels, shards(): pl.pallas_call(settle, out_shape=jax.ShapeDtypeStruct(out_shape, BF16), i...  2.39 us

profile of v3, /device:TPU:5, one launch (start us, length us, event | category | flops | bytes accessed | tf_op | source)
XLA Modules:
  0.0 70.8 jit_solution(11452014433336278213)
XLA Ops:
  0.0 68.2 %attend_and_relay.1.src = bf16[4,16,16,1024]{3,2,1,0:T(8,128)(2,1)} custom-call(s32[1,4,4]{2,1,0:T(4,128)} %matches_in.1, s32[1,4]{1,0:T(1,128)} %counts_in.1, bf16[4,2,128,1024]{3,2,1,0:T(8,128)(2,1)} %frames_in.1, bf16[512,1024]{1,0:T(8,128)(2,1)} %bitcast.2, bf16[1024,1024]{1,0:T(8,128)(2,1)} %wq_in.1, bf16[1024,1024]{1,0:T(8,128)(2,1)} %wk_in.1, ...), custom_call_target="tpu_custom_call" | custom-call | flops 15032385536 | bytes 16777216 | tf_op jit(solution)/shard_map/attend_and_relay/pallas_call | solution.py:497
  68.2 2.4 %settle.1 = bf16[4,16,16,1024]{3,2,1,0:T(8,128)(2,1)} custom-call(bf16[4,16,16,1024]{3,2,1,0:T(8,128)(2,1)} %attend_and_relay.1.src), custom_call_target="tpu_custom_call" | custom-call | tf_op jit(solution)/shard_map/settle/pallas_call | solution.py:545

commit v4 on v3

--- a/solution.py
+++ b/solution.py
@@ -179,7 +179,7 @@
         project_queries(half)
         return carry
 
-    lax.fori_loop(0, jnp.where(slow, 2, 1), project_half, 0)
+    lax.fori_loop(0, 2, project_half, 0)
     for key in range(key_count):
         for chunk in range(chunk_count):
             for copy in shared(key, chunk, partners[0][1]):
@@ -287,7 +287,10 @@
         other, bit = jnp.where(half == 0, 1 - top, top) * half_tiles, 1
         while bit < half_tiles:
             mine = lax.rem(source // bit, 2)
-            other = other + (1 - mine if step // bit % 2 else mine) * bit
+            moved = 1 - mine if step // bit % 2 else mine
+            if 2 * bit == half_tiles:
+                moved = jnp.where(half == 0, step // bit % 2, moved)
+            other = other + moved * bit
             bit *= 2
         return other
 
@@ -314,7 +317,7 @@
 
     relay_steps = [step for step in range(half_tiles) if step // 2 % 2]
 
-    def finish_piece(half, frame):
+    def finish_piece(half, frame, hold=None):
         for chunk in range(chunk_count):
             at = slice(chunk * CHUNK, (chunk + 1) * CHUNK)
             update = jnp.dot(context[...], wo[:, at], preferred_element_type=F32)
@@ -331,9 +334,21 @@
                 stage[frame, image_half(half), :, :, at] = mixed.reshape(rows, half_cols, CHUNK).astype(BF16)
 
         if exchange:
-            order = sorted(range(half_tiles), key=lambda step: (step // 2 % 2, -step))
+            order = sorted(range(half_tiles), key=lambda step: (2 * step // half_tiles, step // 2 % 2, -step))
             for step in order:
                 other = partner(half, step)
+                if hold is not None and 2 * step >= half_tiles:
+                    detour = relayed & (step in relay_steps) & (frame < relay_count)
+
+                    @pl.when(detour)
+                    def _():
+                        hand_over(frame, step, other).start()
+
+                    @pl.when(jnp.logical_not(detour | hold))
+                    def _():
+                        send(frame, other, me).start()
+
+                    continue
                 if step in relay_steps and relay_count:
                     detour = relayed & (half == 0) & (frame < relay_count)
 
@@ -370,10 +385,6 @@
             keys.append(block)
             values.append(jnp.where(used(frame, slot), block, 3 * key_count))
 
-        @pl.when((piece == frame_count) & jnp.logical_not(has_far))
-        def _():
-            project_queries(1)
-
         attend(piece, keys, values)
         finish_piece(half, frame)
         if relay_count:
@@ -398,8 +409,19 @@
         return carry
 
     def late_piece(piece, carry):
-        attend(piece, *named(piece, partners[1][1]), late=True)
-        finish_piece(jnp.int32(0), piece)
+        keys, values = named(piece, partners[1][1])
+        attend(piece, keys[-1:], values[-1:], late=True)
+        finish_piece(jnp.int32(0), piece, slow & (side == 1))
+        return carry
+
+    def middle_piece(key, piece, carry):
+        keys, values = named(piece, partners[1][1])
+        attend(piece, keys[key : key + 1], values[key : key + 1], early=True, late=True)
+        return carry
+
+    def held_sends(frame, carry):
+        for step in range(half_tiles // 2, half_tiles):
+            send(frame, partner(0, step), me).start()
         return carry
 
     lax.fori_loop(0, early_count, early_piece, 0)
@@ -409,13 +431,12 @@
         for key in range(key_count):
             halo(key).wait_recv()
             project_stills(1, partners[1][1], key, 1)
-            if key == 0:
-
-                @pl.when(jnp.logical_not(slow))
-                def _():
-                    project_queries(1)
+            if key < key_count - 1:
+                lax.fori_loop(0, early_count, functools.partial(middle_piece, key), 0)
 
     lax.fori_loop(0, early_count, late_piece, 0)
+    if exchange:
+        lax.fori_loop(0, jnp.where(slow & (side == 1), frame_count, 0), held_sends, 0)
     lax.fori_loop(early_count, 2 * frame_count, one_piece, 0)
 
     @pl.when(has_far)

time: 72.1 us -> 69.2 us (0.960)
  the two profiles are of different devices: /device:TPU:5 before, /device:TPU:11 now
where the time goes in v4:
time: 69.2 us; the launch traced here: 69.1 us
  Pallas kernels  69.1 us (100%)
    pallas_call x1, Pallas kernels, shards(): pl.pallas_call(functools.partial(kernel, tiles, exchange), out_shape=jax....  66.7 us
    pallas_call x1, Pallas kernels, shards(): pl.pallas_call(settle, out_shape=jax.ShapeDtypeStruct(out_shape, BF16), i...  2.39 us

profile of v4, /device:TPU:11, one launch (start us, length us, event | category | flops | bytes accessed | tf_op | source)
XLA Modules:
  0.0 69.1 jit_solution(8980387060183360025)
XLA Ops:
  0.0 66.7 %attend_and_relay.1.src = bf16[4,16,16,1024]{3,2,1,0:T(8,128)(2,1)} custom-call(s32[1,4,4]{2,1,0:T(4,128)} %matches_in.1, s32[1,4]{1,0:T(1,128)} %counts_in.1, bf16[4,2,128,1024]{3,2,1,0:T(8,128)(2,1)} %frames_in.1, bf16[512,1024]{1,0:T(8,128)(2,1)} %bitcast.2, bf16[1024,1024]{1,0:T(8,128)(2,1)} %wq_in.1, bf16[1024,1024]{1,0:T(8,128)(2,1)} %wk_in.1, ...), custom_call_target="tpu_custom_call" | custom-call | flops 15032385536 | bytes 16777216 | tf_op jit(solution)/shard_map/attend_and_relay/pallas_call | solution.py:518
  66.7 2.4 %settle.1 = bf16[4,16,16,1024]{3,2,1,0:T(8,128)(2,1)} custom-call(bf16[4,16,16,1024]{3,2,1,0:T(8,128)(2,1)} %attend_and_relay.1.src), custom_call_target="tpu_custom_call" | custom-call | tf_op jit(solution)/shard_map/settle/pallas_call | solution.py:566

commit v5 on v4

--- a/solution.py
+++ b/solution.py
@@ -11,6 +11,7 @@
 PAIR = 128
 CHUNK = 512
 FAST_EARLY = 1
+GATHER = 4
 GROUP = 8
 RELAYED = 2
 F32 = jnp.float32
@@ -23,7 +24,7 @@
     out,
     matches, counts, frames, stills, wq, wk, wv, wo, queries, key_table, value_table, context,
     stage, relay, scores_even, scores_odd, max_even, max_odd, early_total, early_max,
-    load_sem, halo_send, halo_recv, near_send, near_recv, relay_recv, relay_send, send_sem, recv_sem, own_sem,
+    gather_sem, lead_sem, open_sem, load_sem, weight_sem, halo_send, halo_recv, near_send, near_recv, relay_recv, relay_send, send_sem, recv_sem, own_sem,
 ):
     _, frame_count, rows, half_cols, model_dim = frames.shape
     piece_len = rows * half_cols
@@ -49,53 +50,65 @@
         pltpu.make_async_copy(src, dst, load_sem.at[i])
         for i, (src, dst) in enumerate(
             [
-                (keys_in, stills.at[0]), (wk_in, wk), (wv_in, wv),
+                (keys_in, stills.at[0]),
                 (frames_in.at[:, :, half_columns(0)], frames.at[0]), (wq_in, wq),
                 (frames_in.at[:, :, half_columns(1)], frames.at[1]), (wo_in, wo),
                 (matches_in, matches), (counts_in, counts),
             ]
         )
     ]
-    for load in loads:
+
+    def weight_load(which, chunk):
+        at = pl.ds(pl.multiple_of(chunk * CHUNK, CHUNK), CHUNK)
+        src, dst = ((wk_in, wk), (wv_in, wv))[which]
+        return pltpu.make_async_copy(src.at[:, at], dst.at[:, at], weight_sem.at[which, chunk])
+
+    loads[0].start()
+    for chunk in range(chunk_count):
+        for which in range(2):
+            weight_load(which, chunk).start()
+    for load in loads[1:]:
         load.start()
 
     barrier = pltpu.get_barrier_semaphore()
 
-    def greet(step, carry):
-        other = lax.rem(me + step, tiles)
+    def signal(semaphore, other):
         pl.semaphore_signal(
-            barrier, inc=1, device_id={"tile": other}, device_id_type=pl.DeviceIdType.MESH
-        )
-        return carry
-
-    lax.fori_loop(1, tiles, greet, 0)
-
-    def fill(block):
-        one = jnp.where(block < 3 * key_count, 1.0, 0.0).astype(BF16)
-        for pair in range(pair_count):
-            value_table[block, :, pl.ds(pair * 2 * PAIR + PAIR, PAIR)] = jnp.full(
-                (block_len, PAIR), 1.0, F32
-            ).astype(BF16) * one
+            semaphore, inc=1, device_id={"tile": other}, device_id_type=pl.DeviceIdType.MESH
+        )
 
     odd = lax.rem(me, 2)
     partners = ((me + 1 - 2 * odd, 2 - 2 * odd), (me - 1 + 2 * odd, 2 * odd))
     far = partners[1][0]
     has_far = (far >= 0) & (far < tiles)
-    place = lax.rem(me, 4)
+    place = lax.rem(me, GATHER)
     inner = (place == 1) | (place == 2)
     slow = inner & (me != 1) & (me != tiles - 2)
     held = has_far & inner & (far != 1) & (far != tiles - 2)
     early_count = jnp.where(has_far, jnp.where(slow, frame_count, FAST_EARLY), 0)
 
-    for key in range(key_count):
-        fill(key_count + key)
-        fill(partners[1][1] * key_count + key)
-    fill(3 * key_count)
-    for pair in range(pair_count):
-        value_table[3 * key_count, :, pl.ds(pair * 2 * PAIR, PAIR)] = jnp.zeros(
-            (block_len, PAIR), BF16
-        )
-    pl.semaphore_wait(barrier, tiles - 1)
+    groups = tiles // GATHER
+    leads = place == 0
+
+    def greet(step, carry):
+        signal(barrier, lax.rem(me + step * GATHER, tiles))
+        return carry
+
+    signal(barrier, partners[0][0])
+
+    @pl.when(has_far)
+    def _():
+        signal(barrier, far)
+
+    @pl.when(leads)
+    def _():
+        lax.fori_loop(1, groups, greet, 0)
+        for step in range(2, GATHER):
+            signal(barrier, me + step)
+
+    value_table[3 * key_count] = jnp.zeros((block_len, model_dim), BF16)
+    known = jnp.where(leads, groups - 1, jnp.where(place >= 2, 1, 0))
+    pl.semaphore_wait(barrier, 1 + jnp.where(has_far, 1, 0) + known)
 
     def halo(key):
         part = pl.ds(key * block_len, block_len)
@@ -113,10 +126,9 @@
         block = position * key_count + key
         own = key_count + key
         narrow = pl.ds(pl.multiple_of(chunk * CHUNK, CHUNK), CHUNK)
-        wide = pl.ds(pl.multiple_of(chunk * 2 * CHUNK, 2 * CHUNK), 2 * CHUNK)
         pieces = (
             (key_table.at[own, narrow], key_table.at[block, narrow]),
-            (value_table.at[own, :, wide], value_table.at[block, :, wide]),
+            (value_table.at[own, :, narrow], value_table.at[block, :, narrow]),
         )
         return [
             pltpu.make_async_remote_copy(
@@ -130,6 +142,12 @@
     @pl.when(has_far & jnp.logical_not(held))
     def _():
         start_halo()
+
+    if exchange:
+
+        @pl.when(jnp.logical_not(leads))
+        def _():
+            signal(gather_sem, me - place)
 
     lane = lax.broadcasted_iota(jnp.int32, (piece_len, CHUNK), 1)
     even = lax.rem(lane, PAIR) < head_dim
@@ -152,6 +170,9 @@
     def project_stills(source, slot, first, count, share=False):
         def step(chunk, carry):
             at = pl.ds(pl.multiple_of(chunk * CHUNK, CHUNK), CHUNK)
+            if share:
+                for which in range(2):
+                    weight_load(which, chunk).wait()
             tokens = stills[source, first * block_len : (first + count) * block_len, :]
             k = jnp.dot(tokens, wk[:, at], preferred_element_type=F32).astype(BF16)
             v = jnp.dot(tokens, wv[:, at], preferred_element_type=F32).astype(BF16)
@@ -159,9 +180,7 @@
                 part = slice(key * block_len, (key + 1) * block_len)
                 block = slot * key_count + first + key
                 key_table[block, at, :] = k[part].T
-                for pair in range(CHUNK // PAIR):
-                    to = pl.multiple_of(chunk * 2 * CHUNK + pair * 2 * PAIR, PAIR)
-                    value_table[block, :, pl.ds(to, PAIR)] = v[part, pair * PAIR : (pair + 1) * PAIR]
+                value_table[block, :, at] = v[part]
                 if share:
                     for copy in shared(key, chunk, partners[1][1]):
                         copy.start()
@@ -169,10 +188,21 @@
 
         lax.fori_loop(0, chunk_count, step, 0)
 
-    for load in loads[:3]:
-        load.wait()
+    loads[0].wait()
     project_stills(0, 1, 0, key_count, share=True)
-    for load in loads[3:]:
+
+    def tell(step, carry):
+        signal(lead_sem, lax.rem(me + step * GATHER, tiles))
+        return carry
+
+    if exchange:
+
+        @pl.when(leads)
+        def _():
+            pl.semaphore_wait(gather_sem, GATHER - 1)
+            lax.fori_loop(1, groups, tell, 0)
+
+    for load in loads[1:]:
         load.wait()
 
     def project_half(half, carry):
@@ -180,6 +210,14 @@
         return carry
 
     lax.fori_loop(0, 2, project_half, 0)
+    if exchange:
+
+        @pl.when(leads)
+        def _():
+            pl.semaphore_wait(lead_sem, groups - 1)
+            for step in range(1, GATHER):
+                signal(open_sem, me + step)
+
     for key in range(key_count):
         for chunk in range(chunk_count):
             for copy in shared(key, chunk, partners[0][1]):
@@ -203,6 +241,11 @@
         )
 
     def attend(piece, keys, values, early=False, late=False):
+        ones = [
+            jnp.full((block_len, PAIR), jnp.where(block < 3 * key_count, 1.0, 0.0), F32).astype(BF16)
+            for block in values
+        ]
+
         def score_block(q, slot, at, scores, most):
             s = jnp.dot(q, key_table[keys[slot], at, :], preferred_element_type=F32)
             scores[:, slot * block_len : (slot + 1) * block_len] = s
@@ -211,15 +254,16 @@
                 most = some if most is None else jnp.maximum(most, some)
             return most
 
-        def value_block(slot, wide, scores, most, total):
+        def value_block(slot, at, scores, most, total):
             p = jnp.concatenate(
                 [
-                    jnp.exp(scores[:, at : at + PAIR] - most).astype(BF16)
-                    for at in range(slot * block_len, (slot + 1) * block_len, PAIR)
+                    jnp.exp(scores[:, part : part + PAIR] - most).astype(BF16)
+                    for part in range(slot * block_len, (slot + 1) * block_len, PAIR)
                 ],
                 axis=1,
             )
-            term = jnp.dot(p, value_table[values[slot], :, wide], preferred_element_type=F32)
+            both = jnp.concatenate([value_table[values[slot], :, at], ones[slot]], axis=1)
+            term = jnp.dot(p, both, preferred_element_type=F32)
             return term if total is None else total + term
 
         def close(most, pair, top):
@@ -242,7 +286,7 @@
                 total = early_total[piece, pair] * jnp.concatenate([scale, scale], axis=1)
             for slot in range(len(keys)):
                 next_most = score_block(q, slot, columns(next_pair, PAIR), next_scores, next_most)
-                total = value_block(slot, columns(pair, 2 * PAIR), scores, most, total)
+                total = value_block(slot, columns(pair, PAIR), scores, most, total)
             close(next_most, next_pair, next_top)
             if early:
                 early_total[piece, pair] = total
@@ -425,6 +469,12 @@
         return carry
 
     lax.fori_loop(0, early_count, early_piece, 0)
+    if exchange:
+
+        @pl.when(jnp.logical_not(leads))
+        def _():
+            pl.semaphore_wait(open_sem, 1)
+
 
     @pl.when(has_far)
     def _():
@@ -505,7 +555,7 @@
     piece_len = row_count * half_cols
     slots = matches.shape[2]
     cols = col_count // tiles
-    exchange = cols % 8 == 0 and tiles & (tiles - 1) == 0
+    exchange = cols % 8 == 0 and tiles & (tiles - 1) == 0 and tiles >= 8
     if exchange:
         out_shape = (frame_count, tiles, row_count * cols, model_dim)
         stage_shape = out_shape
@@ -528,7 +578,7 @@
             weight, weight, weight, weight,
             pltpu.VMEM((2 * frame_count, 2 * piece_len, model_dim), BF16),
             pltpu.VMEM((3 * key_count, model_dim, block_len), BF16),
-            pltpu.VMEM((3 * key_count + 1, block_len, 2 * model_dim), BF16),
+            pltpu.VMEM((3 * key_count + 1, block_len, model_dim), BF16),
             pltpu.VMEM((piece_len, model_dim), BF16),
             pltpu.VMEM(stage_shape, BF16),
             pltpu.VMEM((min(RELAYED, frame_count), 4) + stage_shape[2:], BF16),
@@ -538,7 +588,11 @@
             pltpu.VMEM((2 * piece_len, PAIR), F32),
             pltpu.VMEM((frame_count, HEADS // 2, 2 * piece_len, 2 * PAIR), F32),
             pltpu.VMEM((frame_count, HEADS // 2, 2 * piece_len, PAIR), F32),
-            pltpu.SemaphoreType.DMA((9,)),
+            pltpu.SemaphoreType.REGULAR,
+            pltpu.SemaphoreType.REGULAR,
+            pltpu.SemaphoreType.REGULAR,
+            pltpu.SemaphoreType.DMA((7,)),
+            pltpu.SemaphoreType.DMA((2, model_dim // CHUNK)),
             pltpu.SemaphoreType.DMA((key_count,)),
             pltpu.SemaphoreType.DMA((key_count,)),
             pltpu.SemaphoreType.DMA((2, key_count, model_dim // CHUNK)),

time: 69.2 us -> 69.1 us (level)
  the two profiles are of different devices: /device:TPU:11 before, /device:TPU:9 now
where the time goes in v5:
time: 69.1 us; the launch traced here: 68.9 us
  Pallas kernels  68.9 us (100%)
    pallas_call x1, Pallas kernels, shards(): pl.pallas_call(functools.partial(kernel, tiles, exchange), out_shape=jax....  66.5 us
    pallas_call x1, Pallas kernels, shards(): pl.pallas_call(settle, out_shape=jax.ShapeDtypeStruct(out_shape, BF16), i...  2.39 us

profile of v5, /device:TPU:9, one launch (start us, length us, event | category | flops | bytes accessed | tf_op | source)
XLA Modules:
  0.0 68.9 jit_solution(14612418373440413019)
XLA Ops:
  0.0 66.5 %attend_and_relay.1.src = bf16[4,16,16,1024]{3,2,1,0:T(8,128)(2,1)} custom-call(s32[1,4,4]{2,1,0:T(4,128)} %matches_in.1, s32[1,4]{1,0:T(1,128)} %counts_in.1, bf16[4,2,128,1024]{3,2,1,0:T(8,128)(2,1)} %frames_in.1, bf16[512,1024]{1,0:T(8,128)(2,1)} %bitcast.2, bf16[1024,1024]{1,0:T(8,128)(2,1)} %wq_in.1, bf16[1024,1024]{1,0:T(8,128)(2,1)} %wk_in.1, ...), custom_call_target="tpu_custom_call" | custom-call | flops 15032385536 | bytes 16777216 | tf_op jit(solution)/shard_map/attend_and_relay/pallas_call | solution.py:568
  66.5 2.4 %settle.1 = bf16[4,16,16,1024]{3,2,1,0:T(8,128)(2,1)} custom-call(bf16[4,16,16,1024]{3,2,1,0:T(8,128)(2,1)} %attend_and_relay.1.src), custom_call_target="tpu_custom_call" | custom-call | tf_op jit(solution)/shard_map/settle/pallas_call | solution.py:620

commit v6 on v5

--- a/solution.py
+++ b/solution.py
@@ -13,7 +13,7 @@
 FAST_EARLY = 1
 GATHER = 4
 GROUP = 8
-RELAYED = 2
+RELAYED = (2, 2)
 F32 = jnp.float32
 BF16 = jnp.bfloat16
 
@@ -39,6 +39,7 @@
     cols = half_cols // half_tiles
     me = lax.axis_index("tile")
     side = me // half_tiles
+    relay_limit = jnp.where(side == 0, RELAYED[0], RELAYED[1])
 
     def image_half(half):
         return jnp.where(half == 0, 1 - side, side)
@@ -67,8 +68,6 @@
     for chunk in range(chunk_count):
         for which in range(2):
             weight_load(which, chunk).start()
-    for load in loads[1:]:
-        load.start()
 
     barrier = pltpu.get_barrier_semaphore()
 
@@ -173,6 +172,12 @@
             if share:
                 for which in range(2):
                     weight_load(which, chunk).wait()
+
+                @pl.when(chunk == 0)
+                def _():
+                    for load in loads[1:]:
+                        load.start()
+
             tokens = stills[source, first * block_len : (first + count) * block_len, :]
             k = jnp.dot(tokens, wk[:, at], preferred_element_type=F32).astype(BF16)
             v = jnp.dot(tokens, wv[:, at], preferred_element_type=F32).astype(BF16)
@@ -361,6 +366,9 @@
 
     relay_steps = [step for step in range(half_tiles) if step // 2 % 2]
 
+    def waits(step):
+        return lax.rem(me // 2, 2) != step // 2 % 2
+
     def finish_piece(half, frame, hold=None):
         for chunk in range(chunk_count):
             at = slice(chunk * CHUNK, (chunk + 1) * CHUNK)
@@ -381,20 +389,20 @@
             order = sorted(range(half_tiles), key=lambda step: (2 * step // half_tiles, step // 2 % 2, -step))
             for step in order:
                 other = partner(half, step)
-                if hold is not None and 2 * step >= half_tiles:
-                    detour = relayed & (step in relay_steps) & (frame < relay_count)
+                if hold is not None:
+                    detour = relayed & (step in relay_steps) & (frame < relay_limit)
 
                     @pl.when(detour)
                     def _():
                         hand_over(frame, step, other).start()
 
-                    @pl.when(jnp.logical_not(detour | hold))
+                    @pl.when(jnp.logical_not(detour | (hold & waits(step))))
                     def _():
                         send(frame, other, me).start()
 
                     continue
                 if step in relay_steps and relay_count:
-                    detour = relayed & (half == 0) & (frame < relay_count)
+                    detour = relayed & (half == 0) & (frame < relay_limit)
 
                     @pl.when(detour)
                     def _():
@@ -433,7 +441,7 @@
         finish_piece(half, frame)
         if relay_count:
 
-            @pl.when(relays & (piece >= 1) & (piece <= relay_count))
+            @pl.when(relays & (piece >= 1) & (piece <= relay_limit))
             def _():
                 for step in relay_steps:
                     hand_over(piece - 1, step, me).wait_recv()
@@ -464,8 +472,12 @@
         return carry
 
     def held_sends(frame, carry):
-        for step in range(half_tiles // 2, half_tiles):
-            send(frame, partner(0, step), me).start()
+        for step in range(half_tiles):
+
+            @pl.when(waits(step))
+            def _():
+                send(frame, partner(0, step), me).start()
+
         return carry
 
     lax.fori_loop(0, early_count, early_piece, 0)
@@ -504,8 +516,11 @@
         @pl.when(relays)
         def _():
             for frame in range(relay_count):
-                for step in relay_steps:
-                    pass_on(frame, step).wait_send()
+
+                @pl.when(frame < relay_limit)
+                def _():
+                    for step in relay_steps:
+                        pass_on(frame, step).wait_send()
 
     def finish(frame, carry):
         if exchange:
@@ -581,7 +596,7 @@
             pltpu.VMEM((3 * key_count + 1, block_len, model_dim), BF16),
             pltpu.VMEM((piece_len, model_dim), BF16),
             pltpu.VMEM(stage_shape, BF16),
-            pltpu.VMEM((min(RELAYED, frame_count), 4) + stage_shape[2:], BF16),
+            pltpu.VMEM((min(max(RELAYED), frame_count), 4) + stage_shape[2:], BF16),
             pltpu.VMEM((2 * piece_len, slots * block_len), F32),
             pltpu.VMEM((2 * piece_len, slots * block_len), F32),
             pltpu.VMEM((2 * piece_len, PAIR), F32),
@@ -597,8 +612,8 @@
             pltpu.SemaphoreType.DMA((key_count,)),
             pltpu.SemaphoreType.DMA((2, key_count, model_dim // CHUNK)),
             pltpu.SemaphoreType.DMA((2, key_count, model_dim // CHUNK)),
-            pltpu.SemaphoreType.DMA((min(RELAYED, frame_count), 4)),
-            pltpu.SemaphoreType.DMA((min(RELAYED, frame_count), 4)),
+            pltpu.SemaphoreType.DMA((min(max(RELAYED), frame_count), 4)),
+            pltpu.SemaphoreType.DMA((min(max(RELAYED), frame_count), 4)),
             pltpu.SemaphoreType.DMA((frame_count, tiles)),
             pltpu.SemaphoreType.DMA((frame_count, tiles)),
             pltpu.SemaphoreType.DMA((2, frame_count)),

time: 69.1 us -> 68.6 us (level)
  the two profiles are of different devices: /device:TPU:9 before, /device:TPU:5 now
where the time goes in v6:
time: 68.6 us; the launch traced here: 68.5 us
  Pallas kernels  68.5 us (100%)
    pallas_call x1, Pallas kernels, shards(): pl.pallas_call(functools.partial(kernel, tiles, exchange), out_shape=jax....  66.1 us
    pallas_call x1, Pallas kernels, shards(): pl.pallas_call(settle, out_shape=jax.ShapeDtypeStruct(out_shape, BF16), i...  2.39 us

profile of v6, /device:TPU:5, one launch (start us, length us, event | category | flops | bytes accessed | tf_op | source)
XLA Modules:
  0.0 68.5 jit_solution(5218666222882068752)
XLA Ops:
  0.0 66.1 %attend_and_relay.1.src = bf16[4,16,16,1024]{3,2,1,0:T(8,128)(2,1)} custom-call(s32[1,4,4]{2,1,0:T(4,128)} %matches_in.1, s32[1,4]{1,0:T(1,128)} %counts_in.1, bf16[4,2,128,1024]{3,2,1,0:T(8,128)(2,1)} %frames_in.1, bf16[512,1024]{1,0:T(8,128)(2,1)} %bitcast.2, bf16[1024,1024]{1,0:T(8,128)(2,1)} %wq_in.1, bf16[1024,1024]{1,0:T(8,128)(2,1)} %wk_in.1, ...), custom_call_target="tpu_custom_call" | custom-call | flops 15032385536 | bytes 16777216 | tf_op jit(solution)/shard_map/attend_and_relay/pallas_call | solution.py:583
  66.1 2.4 %settle.1 = bf16[4,16,16,1024]{3,2,1,0:T(8,128)(2,1)} custom-call(bf16[4,16,16,1024]{3,2,1,0:T(8,128)(2,1)} %attend_and_relay.1.src), custom_call_target="tpu_custom_call" | custom-call | tf_op jit(solution)/shard_map/settle/pallas_call | solution.py:635

commit v7 on v6

--- a/solution.py
+++ b/solution.py
@@ -214,14 +214,24 @@
         project_queries(half)
         return carry
 
-    lax.fori_loop(0, 2, project_half, 0)
-    if exchange:
-
-        @pl.when(leads)
-        def _():
-            pl.semaphore_wait(lead_sem, groups - 1)
-            for step in range(1, GATHER):
-                signal(open_sem, me + step)
+    def open_group():
+        pl.semaphore_wait(lead_sem, groups - 1)
+        for step in range(1, GATHER):
+            signal(open_sem, me + step)
+
+    lax.fori_loop(0, 1, project_half, 0)
+    if exchange:
+
+        @pl.when(leads & (side == 1))
+        def _():
+            open_group()
+
+    lax.fori_loop(1, jnp.where(has_far, 2, 1), project_half, 0)
+    if exchange:
+
+        @pl.when(leads & (side == 0))
+        def _():
+            open_group()
 
     for key in range(key_count):
         for chunk in range(chunk_count):
@@ -436,6 +446,10 @@
             block = lax.rem(chosen, 3) * key_count + lax.div(chosen, 3)
             keys.append(block)
             values.append(jnp.where(used(frame, slot), block, 3 * key_count))
+
+        @pl.when((piece == frame_count) & jnp.logical_not(has_far))
+        def _():
+            project_queries(1)
 
         attend(piece, keys, values)
         finish_piece(half, frame)

time: 68.6 us -> 68.3 us (level)
  Pallas kernels: 68.5 us -> 67.6 us
    pallas_call x1, Pallas kernels: 66.1 us -> 65.2 us  [shards(): pl.pallas_call(functools.partial(kernel, tiles, exchange), out_shape=jax....]
where the time goes in v7:
time: 68.3 us; the launch traced here: 67.8 us
  Pallas kernels  67.6 us (99%)
    pallas_call x1, Pallas kernels, shards(): pl.pallas_call(functools.partial(kernel, tiles, exchange), out_shape=jax....  65.2 us
    pallas_call x1, Pallas kernels, shards(): pl.pallas_call(settle, out_shape=jax.ShapeDtypeStruct(out_shape, BF16), i...  2.39 us

profile of v7, /device:TPU:5, one launch (start us, length us, event | category | flops | bytes accessed | tf_op | source)
XLA Modules:
  0.0 67.8 jit_solution(9545246688398607570)
XLA Ops:
  0.0 65.2 %attend_and_relay.1.src = bf16[4,16,16,1024]{3,2,1,0:T(8,128)(2,1)} custom-call(s32[1,4,4]{2,1,0:T(4,128)} %matches_in.1, s32[1,4]{1,0:T(1,128)} %counts_in.1, bf16[4,2,128,1024]{3,2,1,0:T(8,128)(2,1)} %frames_in.1, bf16[512,1024]{1,0:T(8,128)(2,1)} %bitcast.2, bf16[1024,1024]{1,0:T(8,128)(2,1)} %wq_in.1, bf16[1024,1024]{1,0:T(8,128)(2,1)} %wk_in.1, ...), custom_call_target="tpu_custom_call" | custom-call | flops 15032385536 | bytes 16777216 | tf_op jit(solution)/shard_map/attend_and_relay/pallas_call | solution.py:597
  65.2 2.4 %settle.1 = bf16[4,16,16,1024]{3,2,1,0:T(8,128)(2,1)} custom-call(bf16[4,16,16,1024]{3,2,1,0:T(8,128)(2,1)} %attend_and_relay.1.src), custom_call_target="tpu_custom_call" | custom-call | tf_op jit(solution)/shard_map/settle/pallas_call | solution.py:649

commit v8 on v7

--- a/solution.py
+++ b/solution.py
@@ -12,6 +12,7 @@
 CHUNK = 512
 FAST_EARLY = 1
 GATHER = 4
+HOLD_FROM = 1
 GROUP = 8
 RELAYED = (2, 2)
 F32 = jnp.float32
@@ -406,7 +407,7 @@
                     def _():
                         hand_over(frame, step, other).start()
 
-                    @pl.when(jnp.logical_not(detour | (hold & waits(step))))
+                    @pl.when(jnp.logical_not(detour | (hold & waits(step) & (frame >= HOLD_FROM))))
                     def _():
                         send(frame, other, me).start()
 
@@ -512,7 +513,7 @@
 
     lax.fori_loop(0, early_count, late_piece, 0)
     if exchange:
-        lax.fori_loop(0, jnp.where(slow & (side == 1), frame_count, 0), held_sends, 0)
+        lax.fori_loop(HOLD_FROM, jnp.where(slow & (side == 1), frame_count, HOLD_FROM), held_sends, 0)
     lax.fori_loop(early_count, 2 * frame_count, one_piece, 0)
 
     @pl.when(has_far)

time: 68.3 us -> 68.3 us (level)
  no operation moved by 1% of the time
where the time goes in v8:
time: 68.3 us; the launch traced here: 67.8 us
  Pallas kernels  67.6 us (99%)
    pallas_call x1, Pallas kernels, shards(): pl.pallas_call(functools.partial(kernel, tiles, exchange), out_shape=jax....  65.2 us
    pallas_call x1, Pallas kernels, shards(): pl.pallas_call(settle, out_shape=jax.ShapeDtypeStruct(out_shape, BF16), i...  2.39 us

profile of v8, /device:TPU:5, one launch (start us, length us, event | category | flops | bytes accessed | tf_op | source)
XLA Modules:
  0.0 67.8 jit_solution(3566202703864751124)
XLA Ops:
  0.0 65.2 %attend_and_relay.1.src = bf16[4,16,16,1024]{3,2,1,0:T(8,128)(2,1)} custom-call(s32[1,4,4]{2,1,0:T(4,128)} %matches_in.1, s32[1,4]{1,0:T(1,128)} %counts_in.1, bf16[4,2,128,1024]{3,2,1,0:T(8,128)(2,1)} %frames_in.1, bf16[512,1024]{1,0:T(8,128)(2,1)} %bitcast.2, bf16[1024,1024]{1,0:T(8,128)(2,1)} %wq_in.1, bf16[1024,1024]{1,0:T(8,128)(2,1)} %wk_in.1, ...), custom_call_target="tpu_custom_call" | custom-call | flops 15032385536 | bytes 16777216 | tf_op jit(solution)/shard_map/attend_and_relay/pallas_call | solution.py:598
  65.2 2.4 %settle.1 = bf16[4,16,16,1024]{3,2,1,0:T(8,128)(2,1)} custom-call(bf16[4,16,16,1024]{3,2,1,0:T(8,128)(2,1)} %attend_and_relay.1.src), custom_call_target="tpu_custom_call" | custom-call | tf_op jit(solution)/shard_map/settle/pallas_call | solution.py:650

commit v9 on v8

--- a/solution.py
+++ b/solution.py
@@ -654,8 +654,8 @@
             out_specs=pl.BlockSpec(memory_space=pl.ANY),
             scratch_shapes=[
                 pltpu.VMEM(out_shape, BF16),
-                pltpu.SemaphoreType.DMA((frame_count, 2)),
-                pltpu.SemaphoreType.DMA((frame_count, 2)),
+                pltpu.SemaphoreType.DMA((frame_count, 1)),
+                pltpu.SemaphoreType.DMA((frame_count, 1)),
             ],
             name="settle",
         )(mixed)

time: 68.3 us -> 68.3 us (level)
  no operation moved by 1% of the time
where the time goes in v9:
time: 68.3 us; the launch traced here: 67.8 us
  Pallas kernels  67.6 us (99%)
    pallas_call x1, Pallas kernels, shards(): pl.pallas_call(functools.partial(kernel, tiles, exchange), out_shape=jax....  65.2 us
    pallas_call x1, Pallas kernels, shards(): pl.pallas_call(settle, out_shape=jax.ShapeDtypeStruct(out_shape, BF16), i...  2.42 us

profile of v9, /device:TPU:5, one launch (start us, length us, event | category | flops | bytes accessed | tf_op | source)
XLA Modules:
  0.0 67.8 jit_solution(17792862072791891732)
XLA Ops:
  0.0 65.2 %attend_and_relay.1.src = bf16[4,16,16,1024]{3,2,1,0:T(8,128)(2,1)} custom-call(s32[1,4,4]{2,1,0:T(4,128)} %matches_in.1, s32[1,4]{1,0:T(1,128)} %counts_in.1, bf16[4,2,128,1024]{3,2,1,0:T(8,128)(2,1)} %frames_in.1, bf16[512,1024]{1,0:T(8,128)(2,1)} %bitcast.2, bf16[1024,1024]{1,0:T(8,128)(2,1)} %wq_in.1, bf16[1024,1024]{1,0:T(8,128)(2,1)} %wk_in.1, ...), custom_call_target="tpu_custom_call" | custom-call | flops 15032385536 | bytes 16777216 | tf_op jit(solution)/shard_map/attend_and_relay/pallas_call | solution.py:598
  65.2 2.4 %settle.1 = bf16[4,16,16,1024]{3,2,1,0:T(8,128)(2,1)} custom-call(bf16[4,16,16,1024]{3,2,1,0:T(8,128)(2,1)} %attend_and_relay.1.src), custom_call_target="tpu_custom_call" | custom-call | tf_op jit(solution)/shard_map/settle/pallas_call | solution.py:650
